TPU v7x, 32 devices: a whole 2x2x4 slice. The times are simulated.
32 devices in a mesh: dom: 8 (over y, x, core), blk: 4 (over z).
Axes of the slice: x: 2, y: 2, z: 4, core: 2. Of those that a mesh axis runs over, the one named last changes fastest.
Arguments:
- features: bfloat16 [32768, 128], P(('dom', 'blk')), may hold values from -6 to 6
- tile_vals: bfloat16 [2304, 128, 128], P(('dom', 'blk')), may hold values from -0.25 to 0.25
- tile_rows: int32 [32, 72], P(('dom', 'blk')), may hold values from 0 to 7
- tile_cols: int32 [32, 72], P(('dom', 'blk')), may hold values from 0 to 7
- tile_count: int32 [32, 4], P(('dom', 'blk')), may hold values from 1 to 18, as said below
- cut_weights: bfloat16 [32768, 384], P(('dom', 'blk')), may hold values from -0.4375 to 0.4375
- send_idx: int32 [32, 384], P(('dom', 'blk')), may hold values from 0 to 1023
- send_count: int32 [32, 8], P(('dom', 'blk')), may hold values from 0 to 48, as said below
- weight: bfloat16 [128, 256], replicated, may hold values from -0.5 to 0.5
- bias: float32 [256], replicated, may hold values from -3 to 3
- cotangent: bfloat16 [32768, 256], P(('dom', 'blk')), may hold values from -6 to 6
Outputs:
- out_y: bfloat16 [32768, 256], P(('dom', 'blk'))
- grad_x: bfloat16 [32768, 128], P(('dom', 'blk'))
- grad_w: float32 [128, 256], replicated
- grad_b: float32 [256], replicated
Inputs may be any that keep to these rules, and one draw needn't show every extreme that they name: `tile_count`: every device has a source position with exactly 18 live slots; devices differ strongly in their counts. `send_count`: zero toward a device's own group; at each index along blk some group receives exactly 48 rows from every other group.
All inputs are finite; a program needn't handle non-finite values.
Results may differ from a plain program's by a relative error of at most 0.018.
Values may be sent and summed in bfloat16 or wider, within the bound.
A program may use at most 128 MiB of HBM per device.

v0:
```python
import math
import jax
import jax.numpy as jnp
from jax import lax
from jax.sharding import PartitionSpec as P


def pad_piece(piece, tile_side):
    padding = jnp.zeros((tile_side, piece.shape[1]), piece.dtype)
    return jnp.concatenate([padding, piece, padding], axis=0)


def pick_blocks(padded, piece_rows, first_rows, tile_side):
    places = jnp.clip(first_rows + tile_side, 0, piece_rows + tile_side)
    picked = jax.vmap(lambda where_at: lax.dynamic_slice_in_dim(padded, where_at, tile_side, 0))(
        places
    )
    inside = (first_rows > -tile_side) & (first_rows < piece_rows)
    return (picked, inside)


def accumulate(running, tiles_here, picked, target, live, flipped):
    row_blocks = running.shape[0]
    selector = (
        (target[:, None] == jnp.arange(row_blocks, dtype=jnp.int32)[None, :]) & live[:, None]
    ).astype(tiles_here.dtype)
    pattern = "tr,tji,tjf->rif" if flipped else "tr,tij,tjf->rif"
    return running + jnp.einsum(
        pattern, selector, tiles_here, picked, preferred_element_type=jnp.float32
    )


def shards(
    features,
    tile_vals,
    tile_rows,
    tile_cols,
    tile_count,
    cut_weights,
    send_idx,
    send_count,
    weight,
    bias,
    cotangent,
):
    rows_dev, feature_width = features.shape
    tile_side = tile_vals.shape[1]
    blk_size = lax.axis_size("blk")
    dom_size = lax.axis_size("dom")
    position = lax.axis_index("blk")
    row_blocks = rows_dev // tile_side
    slot_count = tile_vals.shape[0] // blk_size
    send_most = send_idx.shape[1] // dom_size
    tiles = tile_vals.reshape(blk_size, slot_count, tile_side, tile_side)
    row_ids = tile_rows.reshape(blk_size, slot_count)
    col_ids = tile_cols.reshape(blk_size, slot_count)
    counts = tile_count.reshape(blk_size)
    slot_ids = jnp.arange(slot_count, dtype=jnp.int32)
    live_all = slot_ids[None, :] < counts[:, None]
    sent_rows = send_idx.reshape(dom_size * send_most)
    sent_live = (
        jnp.arange(send_most, dtype=jnp.int32)[None, :] < send_count.reshape(dom_size)[:, None]
    )
    outgoing = jnp.take(features, sent_rows, axis=0).reshape(dom_size, send_most, feature_width)
    outgoing = jnp.where(sent_live[:, :, None], outgoing, jnp.zeros_like(outgoing))
    received = lax.all_to_all(outgoing, "dom", split_axis=0, concat_axis=0, tiled=True)
    cut_part = jnp.dot(
        cut_weights,
        received.reshape(dom_size * send_most, feature_width),
        preferred_element_type=jnp.float32,
    )
    empty = jnp.zeros((row_blocks, tile_side, feature_width), jnp.float32)
    piece = lax.all_gather(features, "blk", axis=0, tiled=True)
    start = jnp.int32(0)
    piece_rows = piece.shape[0]
    padded = pad_piece(piece, tile_side)

    def one_step(source_step, partial_value):
        source = (position - source_step) % blk_size
        lowest = source * rows_dev
        touches = (lowest < start + piece_rows) & (lowest + rows_dev > start)

        def work(inner):
            firsts = lowest + col_ids[source_step] * tile_side
            picked, inside = pick_blocks(padded, piece_rows, firsts, tile_side)
            return accumulate(
                inner,
                tiles[source_step],
                picked,
                row_ids[source_step],
                inside & live_all[source_step],
                False,
            )

        return lax.cond(touches, work, lambda inner: inner, partial_value)

    intra = lax.fori_loop(0, blk_size, one_step, empty).reshape(rows_dev, feature_width)
    aggregated = (intra + cut_part).astype(jnp.bfloat16)
    pre = jnp.dot(aggregated, weight, preferred_element_type=jnp.float32) + bias
    sigmoid_pre = jax.nn.sigmoid(pre)
    out_y = (pre * sigmoid_pre).astype(jnp.bfloat16)
    dpre = (cotangent.astype(jnp.float32) * sigmoid_pre * (1.0 + pre * (1.0 - sigmoid_pre))).astype(
        jnp.bfloat16
    )
    weight_term = lax.dot_general(
        aggregated, dpre, (((0,), (0,)), ((), ())), preferred_element_type=jnp.float32
    )
    bias_term = jnp.sum(dpre.astype(jnp.float32), axis=0)
    dz_rows = lax.dot_general(
        dpre, weight, (((1,), (1,)), ((), ())), preferred_element_type=jnp.float32
    ).astype(jnp.bfloat16)
    cut_back = lax.dot_general(
        cut_weights, dz_rows, (((0,), (0,)), ((), ())), preferred_element_type=jnp.float32
    ).astype(jnp.bfloat16)
    returned = lax.all_to_all(
        cut_back.reshape(dom_size, send_most, feature_width),
        "dom",
        split_axis=0,
        concat_axis=0,
        tiled=True,
    )
    returned = jnp.where(sent_live[:, :, None], returned.astype(jnp.float32), 0.0)
    cut_grad = (
        jnp.zeros((rows_dev, feature_width), jnp.float32)
        .at[sent_rows]
        .add(returned.reshape(dom_size * send_most, feature_width))
    )
    dz_blocks = dz_rows.reshape(row_blocks, tile_side, feature_width)
    row_total = rows_dev * lax.axis_size("blk")

    def one_panel(panel_idx):
        source_step = (position - panel_idx) % blk_size
        picked = jnp.take(dz_blocks, row_ids[source_step], axis=0)
        return accumulate(
            empty, tiles[source_step], picked, col_ids[source_step], live_all[source_step], True
        )

    panel_ids = jnp.arange(row_total // rows_dev, dtype=jnp.int32)
    intra_grad = lax.psum_scatter(
        lax.map(one_panel, panel_ids).reshape(row_total, feature_width),
        "blk",
        scatter_dimension=0,
        tiled=True,
    )
    weight_sum, bias_sum = lax.psum((weight_term, bias_term), ("dom", "blk"))
    scale = 1.0 / math.sqrt(dom_size * blk_size * rows_dev)
    grad_x = (intra_grad + cut_grad).astype(jnp.bfloat16)
    return (out_y, grad_x, weight_sum * scale, bias_sum * scale)


def solution(mesh):
    in_specs = (
        P(("dom", "blk"), None),
        P(("dom", "blk"), None, None),
        P(("dom", "blk"), None),
        P(("dom", "blk"), None),
        P(("dom", "blk"), None),
        P(("dom", "blk"), None),
        P(("dom", "blk"), None),
        P(("dom", "blk"), None),
        P(),
        P(),
        P(("dom", "blk"), None),
    )
    out_specs = (P(("dom", "blk"), None), P(("dom", "blk"), None), P(), P())
    return jax.shard_map(shards, mesh=mesh, in_specs=in_specs, out_specs=out_specs, check_vma=False)
```

profile of v0, /device:TPU:0, one launch (start us, length us, event | category | flops | bytes accessed | tf_op | source)
XLA Modules:
  0.0 325.4 jit_solution(1108997307019440022)
XLA Ops:
  9.4 2.2 gather_fusion.1
  13.1 5.2 %all-to-all-start = ((bf16[8,48,128]{2,1,0:T(8,128)(2,1)}), bf16[8,48,128]{2,1,0:T(8,128)(2,1)S(1)}, u32[]{:S(2)}, u32[]{:S(2)}) async-start(bf16[8,48,128]{2,1,0:T(8,128)(2,1)} %select_select_fusion), calls=%async_computation | async-start | bytes 196608 | tf_op jit(solution)/shard_map/all_to_all | solution.py:66
  22.4 17.8 %all-gather.2.cloned.1.call-done = bf16[4096,128]{1,0:T(8,128)(2,1)} async-done(((bf16[1024,128]{1,0:T(8,128)(2,1)}), bf16[4096,128]{1,0:T(8,128)(2,1)}) %all-gather.2.cloned.1.call-update) | async-done | bytes 1048592 | tf_op jit(solution)/shard_map/all_gather | solution.py:73
  41.6 99.8 %while.34 = (s32[]{:T(128)}, f32[8,128,128]{1,0,2:T(8,128)S(1)}, s32[]{:T(128)}, s32[4,18]{1,0:T(4,128)S(1)}, bf16[4352,128]{1,0:T(8,128)(2,1)S(1)}, /*index=5*/...) while((s32[]{:T(128)}, f32[8,128,128]{1,0,2:T(8,128)S(1)}, ...), condition=%wide.region_3.4_spmd.clone, body=%wide.region_0.3_spmd.clone.sunk | while | flops 80347744 | bytes 3475381 | solution.py:97
  41.7 24.9 %conditional.3 = (f32[8,128,128]{1,0,2:T(8,128)S(1)}) conditional(s32[]{:T(128)} %convert_element_type.66, f32[8,128,128]{1,0,2:T(8,128)S(1)} %get-tuple-element.590, (s32[]{:T(128)}, s32[]{:T(128)}, s32[4,18]{1,0:T(4,128)S(1)}, bf16[4352,128]{1,0:T(8,128)(2,1)S(1)}, bf16[4,18,128,128]{3,2,1,0:T(8,128)(2,1)}, /*index=5*/s32[4,18]{1,0:T(4,128)S(1)}, ...), branch_computations={%region_1.1_spmd, %region_2.2_spmd} | conditional | flops 80347728 | bytes 3474709 | solution.py:95
  41.9 22.6 %while.32 = (s32[]{:T(128)}, bf16[4352,128]{1,0:T(8,128)(2,1)S(1)}, s32[18,2]{0,1:T(2,128)S(1)}, bf16[18,128,128]{2,1,0:T(8,128)(2,1)S(1)}, s32[]{:T(128)}) while((s32[]{:T(128)}, bf16[4352,128]{1,0:T(8,128)(2,1)S(1)}, s32[18,2]{0,1:T(2,128)S(1)}, bf16[18,128,128]{2,1,0:T(8,128)(2,1)S(1)}, s32[]{:T(128)}) %tuple.94), condition=%wide.while_cond, body=%wide.while_body.sunk | while | flops 2 | bytes 65641 | solution.py:15
  64.5 1.6 fusion.10
  66.6 24.9 %conditional.3 = (f32[8,128,128]{1,0,2:T(8,128)S(1)}) conditional(s32[]{:T(128)} %convert_element_type.66, f32[8,128,128]{1,0,2:T(8,128)S(1)} %get-tuple-element.590, (s32[]{:T(128)}, s32[]{:T(128)}, s32[4,18]{1,0:T(4,128)S(1)}, bf16[4352,128]{1,0:T(8,128)(2,1)S(1)}, bf16[4,18,128,128]{3,2,1,0:T(8,128)(2,1)}, /*index=5*/s32[4,18]{1,0:T(4,128)S(1)}, ...), branch_computations={%region_1.1_spmd, %region_2.2_spmd} | conditional | flops 80347728 | bytes 3474709 | solution.py:95
  66.8 22.6 %while.32 = (s32[]{:T(128)}, bf16[4352,128]{1,0:T(8,128)(2,1)S(1)}, s32[18,2]{0,1:T(2,128)S(1)}, bf16[18,128,128]{2,1,0:T(8,128)(2,1)S(1)}, s32[]{:T(128)}) while((s32[]{:T(128)}, bf16[4352,128]{1,0:T(8,128)(2,1)S(1)}, s32[18,2]{0,1:T(2,128)S(1)}, bf16[18,128,128]{2,1,0:T(8,128)(2,1)S(1)}, s32[]{:T(128)}) %tuple.94), condition=%wide.while_cond, body=%wide.while_body.sunk | while | flops 2 | bytes 65641 | solution.py:15
  89.4 1.6 fusion.10
  91.6 24.9 %conditional.3 = (f32[8,128,128]{1,0,2:T(8,128)S(1)}) conditional(s32[]{:T(128)} %convert_element_type.66, f32[8,128,128]{1,0,2:T(8,128)S(1)} %get-tuple-element.590, (s32[]{:T(128)}, s32[]{:T(128)}, s32[4,18]{1,0:T(4,128)S(1)}, bf16[4352,128]{1,0:T(8,128)(2,1)S(1)}, bf16[4,18,128,128]{3,2,1,0:T(8,128)(2,1)}, /*index=5*/s32[4,18]{1,0:T(4,128)S(1)}, ...), branch_computations={%region_1.1_spmd, %region_2.2_spmd} | conditional | flops 80347728 | bytes 3474709 | solution.py:95
  91.7 22.6 %while.32 = (s32[]{:T(128)}, bf16[4352,128]{1,0:T(8,128)(2,1)S(1)}, s32[18,2]{0,1:T(2,128)S(1)}, bf16[18,128,128]{2,1,0:T(8,128)(2,1)S(1)}, s32[]{:T(128)}) while((s32[]{:T(128)}, bf16[4352,128]{1,0:T(8,128)(2,1)S(1)}, s32[18,2]{0,1:T(2,128)S(1)}, bf16[18,128,128]{2,1,0:T(8,128)(2,1)S(1)}, s32[]{:T(128)}) %tuple.94), condition=%wide.while_cond, body=%wide.while_body.sunk | while | flops 2 | bytes 65641 | solution.py:15
  114.4 1.6 fusion.10
  116.5 24.9 %conditional.3 = (f32[8,128,128]{1,0,2:T(8,128)S(1)}) conditional(s32[]{:T(128)} %convert_element_type.66, f32[8,128,128]{1,0,2:T(8,128)S(1)} %get-tuple-element.590, (s32[]{:T(128)}, s32[]{:T(128)}, s32[4,18]{1,0:T(4,128)S(1)}, bf16[4352,128]{1,0:T(8,128)(2,1)S(1)}, bf16[4,18,128,128]{3,2,1,0:T(8,128)(2,1)}, /*index=5*/s32[4,18]{1,0:T(4,128)S(1)}, ...), branch_computations={%region_1.1_spmd, %region_2.2_spmd} | conditional | flops 80347728 | bytes 3474709 | solution.py:95
  116.7 22.6 %while.32 = (s32[]{:T(128)}, bf16[4352,128]{1,0:T(8,128)(2,1)S(1)}, s32[18,2]{0,1:T(2,128)S(1)}, bf16[18,128,128]{2,1,0:T(8,128)(2,1)S(1)}, s32[]{:T(128)}) while((s32[]{:T(128)}, bf16[4352,128]{1,0:T(8,128)(2,1)S(1)}, s32[18,2]{0,1:T(2,128)S(1)}, bf16[18,128,128]{2,1,0:T(8,128)(2,1)S(1)}, s32[]{:T(128)}) %tuple.94), condition=%wide.while_cond, body=%wide.while_body.sunk | while | flops 2 | bytes 65641 | solution.py:15
  139.3 1.6 fusion.10
  141.8 2.5 convert_reduce_fusion
  145.6 20.2 %while.33 = (s32[]{:T(128)}, f32[4,8,128,128]{3,2,1,0:T(8,128)}, s32[4]{0:T(128)S(1)}, s32[]{:T(128)}, s32[4,18]{1,0:T(4,128)S(1)}, /*index=5*/bf16[8,128,128]{2...) while((s32[]{:T(128)}, f32[4,8,128,128]{3,2,1,0:T(8,128)}, ...), condition=%wide.region_5.6_spmd, body=%wide.region_4.5_spmd.sunk | while | flops 80512464 | bytes 6165470 | solution.py:140
  166.9 3.7 %all-to-all-start.1 = ((bf16[8,48,128]{2,1,0:T(8,128)(2,1)}), bf16[8,48,128]{2,1,0:T(8,128)(2,1)S(1)}, u32[]{:S(2)}, u32[]{:S(2)}) async-start(bf16[8,48,128]{2,1,0:T(8,128)(2,1)} %bitcast.26), calls=%async_computation.2 | async-start | bytes 196608 | tf_op jit(solution)/shard_map/all_to_all | solution.py:115
  170.6 40.6 %psum.15 = f32[256]{0:T(256)S(1)} all-reduce(f32[256]{0:T(256)S(1)} %get-tuple-element.426), channel_id=1, replica_groups=mesh['dom'=8,'blk'=4] {'dom','blk'}, use_global_device_ids=true, to_apply=%region_10.11 | all-reduce | flops 256 | bytes 2048 | tf_op jit(solution)/shard_map/psum | solution.py:145
  211.7 56.0 %all-reduce.3.cloned.1.call-done = f32[128,256]{1,0:T(8,128)} async-done(((f32[128,256]{1,0:T(8,128)}), f32[128,256]{1,0:T(8,128)}) %all-reduce.3.cloned.1.call-update) | async-done | bytes 131088 | tf_op jit(solution)/shard_map/psum | solution.py:145
  269.4 43.5 %reduce-scatter.2.cloned.1.call-done = f32[1024,128]{1,0:T(8,128)} async-done(((f32[4096,128]{1,0:T(8,128)}), f32[1024,128]{1,0:T(8,128)}) %reduce-scatter.2.cloned.1.call-update) | async-done | bytes 524304 | tf_op jit(solution)/shard_map/reduce_scatter | solution.py:139
  312.9 4.2 %scatter_fusion = f32[1024,128]{1,0:T(8,128)} fusion(f32[1024,128]{1,0:T(8,128)} %reduce-scatter.2.cloned.1.call-done, s32[384]{0:T(512)S(1)} %fusion.45, f32[384,128]{1,0:T(8,128)S(1)} %bitcast.102), kind=kCustom, calls=%fused_computation.2 | custom fusion | flops 49152 | bytes 591360 | tf_op jit(solution)/shard_map/scatter-add | solution.py:126
  317.1 1.8 convert_element_type.50
  (333 shorter events, 122.7 us)
Async XLA Ops:
  7.2 134.2 %copy-start = (bf16[1024,384]{1,0:T(8,128)(2,1)S(1)}, bf16[1024,384]{1,0:T(8,128)(2,1)}, u32[]{:S(2)}) copy-start(bf16[1024,384]{1,0:T(8,128)(2,1)} %param.22) | copy-start | bytes 2359300
  7.2 33.1 %all-gather.2.cloned.1.call-start = ((), (), s32[]{:S(2)}) async-start(), calls=%async_computation.3 | async-start | bytes 1310720 | tf_op jit(solution)/shard_map/all_gather | solution.py:73
  7.9 33.7 %copy-start.2 = (s32[1,4]{1,0:T(1,128)S(1)}, s32[1,4]{1,0:T(1,128)}, u32[]{:S(2)}) copy-start(s32[1,4]{1,0:T(1,128)} %param.21) | copy-start | bytes 52
  13.1 128.3 %all-to-all-start = ((bf16[8,48,128]{2,1,0:T(8,128)(2,1)}), bf16[8,48,128]{2,1,0:T(8,128)(2,1)S(1)}, u32[]{:S(2)}, u32[]{:S(2)}) async-start(bf16[8,48,128]{2,1,0:T(8,128)(2,1)} %select_select_fusion), calls=%async_computation | async-start | bytes 196608 | tf_op jit(solution)/shard_map/all_to_all | solution.py:66
  18.3 249.4 %all-reduce.3.cloned.1.call-start = ((), (), s32[]{:S(2)}) async-start(), calls=%async_computation.5 | async-start | bytes 262144 | tf_op jit(solution)/shard_map/psum | solution.py:145
  41.6 100.2 %copy-start.1 = (bf16[128,256]{1,0:T(8,128)(2,1)S(1)}, bf16[128,256]{1,0:T(8,128)(2,1)}, u32[]{:S(2)}) copy-start(bf16[128,256]{1,0:T(8,128)(2,1)} %param.25) | copy-start | bytes 196612
  41.6 100.2 %copy-start.3 = (f32[256]{0:T(256)S(1)}, f32[256]{0:T(256)}, u32[]{:S(2)}) copy-start(f32[256]{0:T(256)} %param.26) | copy-start | bytes 3076
  145.6 167.3 %reduce-scatter.2.cloned.1.call-start = ((), (), s32[]{:S(2)}) async-start(), calls=%async_computation.4 | async-start | bytes 2621440 | tf_op jit(solution)/shard_map/reduce_scatter | solution.py:139
  166.9 102.3 %all-to-all-start.1 = ((bf16[8,48,128]{2,1,0:T(8,128)(2,1)}), bf16[8,48,128]{2,1,0:T(8,128)(2,1)S(1)}, u32[]{:S(2)}, u32[]{:S(2)}) async-start(bf16[8,48,128]{2,1,0:T(8,128)(2,1)} %bitcast.26), calls=%async_computation.2 | async-start | bytes 196608 | tf_op jit(solution)/shard_map/all_to_all | solution.py:115
Sparse Core Ops, SparseCore 0:
  9.6 30.6 all-gather.1
  145.7 121.9 all-reduce.2
  270.0 42.8 reduce-scatter.1
where the time goes:
time: 327 us; the launch traced here: 325 us
  waiting for transfers between devices  118 us (36%)
  local copies, waits for them, and re-layouts  102 us (31%)
  blocking collectives  40.6 us (12%)
  matrix products  20.5 us (6%)
  other arithmetic  16.4 us (5%)
  between operations  13.9 us (4%)
  starting transfers between devices  8.96 us (3%)
  loops' own time  4.92 us (2%)
    gather x216, local copies, waits for them, and re-layouts  89 us
    psum x1, waiting for transfers between devices, shards(): weight_sum, bias_sum = lax.psum((weight_term, bias_term), ('dom', 'blk'))  56 us
    reduce_scatter x1, waiting for transfers between devices, shards(): lax.psum_scatter(lax.map(one_panel, panel_ids).reshape(row_total, feature...  43.5 us
    psum x1, blocking collectives, shards(): weight_sum, bias_sum = lax.psum((weight_term, bias_term), ('dom', 'blk'))  40.6 us
    all_gather x1, waiting for transfers between devices, shards(): piece = lax.all_gather(features, 'blk', axis=0, tiled=True)  17.8 us
    dot_general x16, matrix products, accumulate(): jnp.einsum(pattern, selector, tiles_here, picked, preferred_element_type=...  16 us
  transfers between devices with their start and end apart: 5, of which 3 were waited for; matrix products, arithmetic and copies ran while one was open for 40% of the time, Pallas kernels for 0%

commit v1 on v0

--- a/solution.py
+++ b/solution.py
@@ -142,7 +142,9 @@
         scatter_dimension=0,
         tiled=True,
     )
-    weight_sum, bias_sum = lax.psum((weight_term, bias_term), ("dom", "blk"))
+    weight_sum, bias_sum = lax.psum(
+        lax.psum((weight_term, bias_term), axis_name="blk"), axis_name="dom"
+    )
     scale = 1.0 / math.sqrt(dom_size * blk_size * rows_dev)
     grad_x = (intra_grad + cut_grad).astype(jnp.bfloat16)
     return (out_y, grad_x, weight_sum * scale, bias_sum * scale)

time: 327 us -> 295 us (0.902)
  blocking collectives: 40.6 us -> 22.9 us
  waiting for transfers between devices: 118 us -> 104 us
    psum x1 -> x2, blocking collectives: 40.6 us -> 22.9 us  [the longest x1 12.4 us: shards(): lax.psum(lax.psum((weight_term, bias_term), axis_name='blk'), axis_name='...]
    psum x1 -> x2, waiting for transfers between devices: 56 us -> 41.2 us  [the longest x1 33.7 us: shards(): lax.psum((weight_term, bias_term), axis_name='blk')]
  transfers between devices with their start and end apart: 5 -> 6, of which waited for: 3 -> 4; matrix products, arithmetic and copies ran while one was open for 40% -> 44% of each run, Pallas kernels for 0% -> 0%
where the time goes in v1:
time: 295 us; the launch traced here: 293 us
  waiting for transfers between devices  104 us (35%)
  local copies, waits for them, and re-layouts  102 us (35%)
  blocking collectives  22.9 us (8%)
  matrix products  20.5 us (7%)
  other arithmetic  16.4 us (6%)
  between operations  13.9 us (5%)
  starting transfers between devices  8.92 us (3%)
  loops' own time  4.92 us (2%)
    gather x216, local copies, waits for them, and re-layouts  89 us
    reduce_scatter x1, waiting for transfers between devices, shards(): lax.psum_scatter(lax.map(one_panel, panel_ids).reshape(row_total, feature...  43.8 us
    psum x1, waiting for transfers between devices, shards(): lax.psum((weight_term, bias_term), axis_name='blk')  33.7 us
    all_gather x1, waiting for transfers between devices, shards(): piece = lax.all_gather(features, 'blk', axis=0, tiled=True)  17.8 us
    dot_general x16, matrix products, accumulate(): jnp.einsum(pattern, selector, tiles_here, picked, preferred_element_type=...  16 us
    psum x1, blocking collectives, shards(): lax.psum(lax.psum((weight_term, bias_term), axis_name='blk'), axis_name='...  12.4 us
    psum x1, blocking collectives, shards(): lax.psum((weight_term, bias_term), axis_name='blk')  10.5 us
    psum x1, waiting for transfers between devices, shards(): lax.psum(lax.psum((weight_term, bias_term), axis_name='blk'), axis_name='...  7.46 us
  transfers between devices with their start and end apart: 6, of which 4 were waited for; matrix products, arithmetic and copies ran while one was open for 44% of the time, Pallas kernels for 0%

profile of v1, /device:TPU:0, one launch (start us, length us, event | category | flops | bytes accessed | tf_op | source)
XLA Modules:
  0.0 293.3 jit_solution(17038252428437830140)
XLA Ops:
  9.4 2.2 gather_fusion.1
  13.1 5.2 %all-to-all-start = ((bf16[8,48,128]{2,1,0:T(8,128)(2,1)}), bf16[8,48,128]{2,1,0:T(8,128)(2,1)S(1)}, u32[]{:S(2)}, u32[]{:S(2)}) async-start(bf16[8,48,128]{2,1,0:T(8,128)(2,1)} %select_select_fusion), calls=%async_computation | async-start | bytes 196608 | tf_op jit(solution)/shard_map/all_to_all | solution.py:66
  22.4 17.8 %all-gather.2.cloned.1.call-done = bf16[4096,128]{1,0:T(8,128)(2,1)} async-done(((bf16[1024,128]{1,0:T(8,128)(2,1)}), bf16[4096,128]{1,0:T(8,128)(2,1)}) %all-gather.2.cloned.1.call-update) | async-done | bytes 1048592 | tf_op jit(solution)/shard_map/all_gather | solution.py:73
  41.6 99.8 %while.34 = (s32[]{:T(128)}, f32[8,128,128]{1,0,2:T(8,128)S(1)}, s32[]{:T(128)}, s32[4,18]{1,0:T(4,128)S(1)}, bf16[4352,128]{1,0:T(8,128)(2,1)S(1)}, /*index=5*/...) while((s32[]{:T(128)}, f32[8,128,128]{1,0,2:T(8,128)S(1)}, ...), condition=%wide.region_3.4_spmd.clone, body=%wide.region_0.3_spmd.clone.sunk | while | flops 80347744 | bytes 3475381 | solution.py:97
  41.7 24.9 %conditional.3 = (f32[8,128,128]{1,0,2:T(8,128)S(1)}) conditional(s32[]{:T(128)} %convert_element_type.66, f32[8,128,128]{1,0,2:T(8,128)S(1)} %get-tuple-element.590, (s32[]{:T(128)}, s32[]{:T(128)}, s32[4,18]{1,0:T(4,128)S(1)}, bf16[4352,128]{1,0:T(8,128)(2,1)S(1)}, bf16[4,18,128,128]{3,2,1,0:T(8,128)(2,1)}, /*index=5*/s32[4,18]{1,0:T(4,128)S(1)}, ...), branch_computations={%region_1.1_spmd, %region_2.2_spmd} | conditional | flops 80347728 | bytes 3474709 | solution.py:95
  41.9 22.6 %while.32 = (s32[]{:T(128)}, bf16[4352,128]{1,0:T(8,128)(2,1)S(1)}, s32[18,2]{0,1:T(2,128)S(1)}, bf16[18,128,128]{2,1,0:T(8,128)(2,1)S(1)}, s32[]{:T(128)}) while((s32[]{:T(128)}, bf16[4352,128]{1,0:T(8,128)(2,1)S(1)}, s32[18,2]{0,1:T(2,128)S(1)}, bf16[18,128,128]{2,1,0:T(8,128)(2,1)S(1)}, s32[]{:T(128)}) %tuple.94), condition=%wide.while_cond, body=%wide.while_body.sunk | while | flops 2 | bytes 65641 | solution.py:15
  66.6 24.9 %conditional.3 = (f32[8,128,128]{1,0,2:T(8,128)S(1)}) conditional(s32[]{:T(128)} %convert_element_type.66, f32[8,128,128]{1,0,2:T(8,128)S(1)} %get-tuple-element.590, (s32[]{:T(128)}, s32[]{:T(128)}, s32[4,18]{1,0:T(4,128)S(1)}, bf16[4352,128]{1,0:T(8,128)(2,1)S(1)}, bf16[4,18,128,128]{3,2,1,0:T(8,128)(2,1)}, /*index=5*/s32[4,18]{1,0:T(4,128)S(1)}, ...), branch_computations={%region_1.1_spmd, %region_2.2_spmd} | conditional | flops 80347728 | bytes 3474709 | solution.py:95
  66.8 22.6 %while.32 = (s32[]{:T(128)}, bf16[4352,128]{1,0:T(8,128)(2,1)S(1)}, s32[18,2]{0,1:T(2,128)S(1)}, bf16[18,128,128]{2,1,0:T(8,128)(2,1)S(1)}, s32[]{:T(128)}) while((s32[]{:T(128)}, bf16[4352,128]{1,0:T(8,128)(2,1)S(1)}, s32[18,2]{0,1:T(2,128)S(1)}, bf16[18,128,128]{2,1,0:T(8,128)(2,1)S(1)}, s32[]{:T(128)}) %tuple.94), condition=%wide.while_cond, body=%wide.while_body.sunk | while | flops 2 | bytes 65641 | solution.py:15
  89.4 1.6 fusion.10
  91.6 24.9 %conditional.3 = (f32[8,128,128]{1,0,2:T(8,128)S(1)}) conditional(s32[]{:T(128)} %convert_element_type.66, f32[8,128,128]{1,0,2:T(8,128)S(1)} %get-tuple-element.590, (s32[]{:T(128)}, s32[]{:T(128)}, s32[4,18]{1,0:T(4,128)S(1)}, bf16[4352,128]{1,0:T(8,128)(2,1)S(1)}, bf16[4,18,128,128]{3,2,1,0:T(8,128)(2,1)}, /*index=5*/s32[4,18]{1,0:T(4,128)S(1)}, ...), branch_computations={%region_1.1_spmd, %region_2.2_spmd} | conditional | flops 80347728 | bytes 3474709 | solution.py:95
  91.7 22.6 %while.32 = (s32[]{:T(128)}, bf16[4352,128]{1,0:T(8,128)(2,1)S(1)}, s32[18,2]{0,1:T(2,128)S(1)}, bf16[18,128,128]{2,1,0:T(8,128)(2,1)S(1)}, s32[]{:T(128)}) while((s32[]{:T(128)}, bf16[4352,128]{1,0:T(8,128)(2,1)S(1)}, s32[18,2]{0,1:T(2,128)S(1)}, bf16[18,128,128]{2,1,0:T(8,128)(2,1)S(1)}, s32[]{:T(128)}) %tuple.94), condition=%wide.while_cond, body=%wide.while_body.sunk | while | flops 2 | bytes 65641 | solution.py:15
  116.5 24.9 %conditional.3 = (f32[8,128,128]{1,0,2:T(8,128)S(1)}) conditional(s32[]{:T(128)} %convert_element_type.66, f32[8,128,128]{1,0,2:T(8,128)S(1)} %get-tuple-element.590, (s32[]{:T(128)}, s32[]{:T(128)}, s32[4,18]{1,0:T(4,128)S(1)}, bf16[4352,128]{1,0:T(8,128)(2,1)S(1)}, bf16[4,18,128,128]{3,2,1,0:T(8,128)(2,1)}, /*index=5*/s32[4,18]{1,0:T(4,128)S(1)}, ...), branch_computations={%region_1.1_spmd, %region_2.2_spmd} | conditional | flops 80347728 | bytes 3474709 | solution.py:95
  116.7 22.6 %while.32 = (s32[]{:T(128)}, bf16[4352,128]{1,0:T(8,128)(2,1)S(1)}, s32[18,2]{0,1:T(2,128)S(1)}, bf16[18,128,128]{2,1,0:T(8,128)(2,1)S(1)}, s32[]{:T(128)}) while((s32[]{:T(128)}, bf16[4352,128]{1,0:T(8,128)(2,1)S(1)}, s32[18,2]{0,1:T(2,128)S(1)}, bf16[18,128,128]{2,1,0:T(8,128)(2,1)S(1)}, s32[]{:T(128)}) %tuple.94), condition=%wide.while_cond, body=%wide.while_body.sunk | while | flops 2 | bytes 65641 | solution.py:15
  139.3 1.6 fusion.10
  141.8 2.5 convert_reduce_fusion
  145.6 33.7 %all-reduce.4.cloned.1.call-done = f32[128,256]{1,0:T(8,128)} async-done(((f32[128,256]{1,0:T(8,128)}), f32[128,256]{1,0:T(8,128)}) %all-reduce.4.cloned.1.call-update) | async-done | bytes 131088 | tf_op jit(solution)/shard_map/psum | solution.py:146
  179.5 20.2 %while.33 = (s32[]{:T(128)}, f32[4,8,128,128]{3,2,1,0:T(8,128)}, s32[4]{0:T(128)S(1)}, s32[]{:T(128)}, s32[4,18]{1,0:T(4,128)S(1)}, /*index=5*/bf16[8,128,128]{2...) while((s32[]{:T(128)}, f32[4,8,128,128]{3,2,1,0:T(8,128)}, ...), condition=%wide.region_5.6_spmd, body=%wide.region_4.5_spmd.sunk | while | flops 80512464 | bytes 6165470 | solution.py:140
  200.7 3.6 %all-to-all-start.1 = ((bf16[8,48,128]{2,1,0:T(8,128)(2,1)}), bf16[8,48,128]{2,1,0:T(8,128)(2,1)S(1)}, u32[]{:S(2)}, u32[]{:S(2)}) async-start(bf16[8,48,128]{2,1,0:T(8,128)(2,1)} %bitcast.26), calls=%async_computation.2 | async-start | bytes 196608 | tf_op jit(solution)/shard_map/all_to_all | solution.py:115
  204.3 10.5 %psum.30 = f32[256]{0:T(256)S(1)} all-reduce(f32[256]{0:T(256)S(1)} %get-tuple-element.426), channel_id=1, replica_groups=mesh['dom'=8,'blk'=4] {'blk'}, use_global_device_ids=true, to_apply=%region_11.12 | all-reduce | flops 256 | bytes 2048 | tf_op jit(solution)/shard_map/psum | solution.py:146
  214.8 12.4 %psum.31 = f32[256]{0:T(256)S(1)} all-reduce(f32[256]{0:T(256)S(1)} %psum.30), channel_id=1, replica_groups=mesh['dom'=8,'blk'=4] {'dom'}, use_global_device_ids=true, to_apply=%region_12.13 | all-reduce | flops 256 | bytes 2048 | tf_op jit(solution)/shard_map/psum | solution.py:145
  227.9 7.5 %all-reduce.6.cloned.1.call-done = f32[128,256]{1,0:T(8,128)} async-done(((f32[128,256]{1,0:T(8,128)}), f32[128,256]{1,0:T(8,128)}) %all-reduce.6.cloned.1.call-update) | async-done | bytes 131088 | tf_op jit(solution)/shard_map/psum | solution.py:145
  236.9 43.8 %reduce-scatter.2.cloned.1.call-done = f32[1024,128]{1,0:T(8,128)} async-done(((f32[4096,128]{1,0:T(8,128)}), f32[1024,128]{1,0:T(8,128)}) %reduce-scatter.2.cloned.1.call-update) | async-done | bytes 524304 | tf_op jit(solution)/shard_map/reduce_scatter | solution.py:139
  280.8 4.2 %scatter_fusion = f32[1024,128]{1,0:T(8,128)} fusion(f32[1024,128]{1,0:T(8,128)} %reduce-scatter.2.cloned.1.call-done, s32[384]{0:T(512)S(1)} %fusion.45, f32[384,128]{1,0:T(8,128)S(1)} %bitcast.102), kind=kCustom, calls=%fused_computation.2 | custom fusion | flops 49152 | bytes 591360 | tf_op jit(solution)/shard_map/scatter-add | solution.py:126
  285.0 1.8 convert_element_type.50
  (337 shorter events, 126.0 us)
Async XLA Ops:
  7.2 134.2 %copy-start = (bf16[1024,384]{1,0:T(8,128)(2,1)S(1)}, bf16[1024,384]{1,0:T(8,128)(2,1)}, u32[]{:S(2)}) copy-start(bf16[1024,384]{1,0:T(8,128)(2,1)} %param.22) | copy-start | bytes 2359300
  7.2 33.1 %all-gather.2.cloned.1.call-start = ((), (), s32[]{:S(2)}) async-start(), calls=%async_computation.3 | async-start | bytes 1310720 | tf_op jit(solution)/shard_map/all_gather | solution.py:73
  7.9 33.7 %copy-start.2 = (s32[1,4]{1,0:T(1,128)S(1)}, s32[1,4]{1,0:T(1,128)}, u32[]{:S(2)}) copy-start(s32[1,4]{1,0:T(1,128)} %param.21) | copy-start | bytes 52
  13.1 128.3 %all-to-all-start = ((bf16[8,48,128]{2,1,0:T(8,128)(2,1)}), bf16[8,48,128]{2,1,0:T(8,128)(2,1)S(1)}, u32[]{:S(2)}, u32[]{:S(2)}) async-start(bf16[8,48,128]{2,1,0:T(8,128)(2,1)} %select_select_fusion), calls=%async_computation | async-start | bytes 196608 | tf_op jit(solution)/shard_map/all_to_all | solution.py:66
  18.3 161.1 %all-reduce.4.cloned.1.call-start = ((), (), s32[]{:S(2)}) async-start(), calls=%async_computation.5 | async-start | bytes 262144 | tf_op jit(solution)/shard_map/psum | solution.py:146
  41.6 100.2 %copy-start.1 = (bf16[128,256]{1,0:T(8,128)(2,1)S(1)}, bf16[128,256]{1,0:T(8,128)(2,1)}, u32[]{:S(2)}) copy-start(bf16[128,256]{1,0:T(8,128)(2,1)} %param.25) | copy-start | bytes 196612
  41.6 100.2 %copy-start.3 = (f32[256]{0:T(256)S(1)}, f32[256]{0:T(256)}, u32[]{:S(2)}) copy-start(f32[256]{0:T(256)} %param.26) | copy-start | bytes 3076
  145.3 90.1 %all-reduce.6.cloned.1.call-start = ((), (), s32[]{:S(2)}) async-start(), calls=%async_computation.6 | async-start | bytes 262144 | tf_op jit(solution)/shard_map/psum | solution.py:145
  179.4 101.4 %reduce-scatter.2.cloned.1.call-start = ((), (), s32[]{:S(2)}) async-start(), calls=%async_computation.4 | async-start | bytes 2621440 | tf_op jit(solution)/shard_map/reduce_scatter | solution.py:139
  200.7 27.0 %all-to-all-start.1 = ((bf16[8,48,128]{2,1,0:T(8,128)(2,1)}), bf16[8,48,128]{2,1,0:T(8,128)(2,1)S(1)}, u32[]{:S(2)}, u32[]{:S(2)}) async-start(bf16[8,48,128]{2,1,0:T(8,128)(2,1)} %bitcast.26), calls=%async_computation.2 | async-start | bytes 196608 | tf_op jit(solution)/shard_map/all_to_all | solution.py:115
Sparse Core Ops, SparseCore 0:
  9.6 30.6 all-gather.1
  145.4 33.9 all-reduce.3
  182.7 52.6 all-reduce.5
  237.5 43.2 reduce-scatter.1
